TPU v7x, 32 devices: a whole 2x2x4 slice. The times are simulated.
32 devices in a mesh: groups: 2 (over x), row: 8 (over z, y), col: 2 (over core).
Axes of the slice: x: 2, y: 2, z: 4, core: 2. Of those that a mesh axis runs over, the one named last changes fastest.
Arguments:
- tokens: bfloat16 [768, 6144], P(('groups', 'row'), 'col'), parts along dimension 0, may hold values from -400 to 400, as said below
- norm_gain: float32 [6144], P('col'), may hold values from 0.1 to 1.9
- norm_bias: float32 [6144], P('col'), may hold values from -3 to 3
- up_weight: bfloat16 [6144, 24576], P('col', 'row'), may hold values from -0.078125 to 0.078125
- up_bias: float32 [24576], P('row'), may hold values from -3 to 3
- down_weight: bfloat16 [24576, 6144], P('row', 'col'), may hold values from -0.0390625 to 0.0390625
- down_bias: float32 [6144], P('col'), may hold values from -3 to 3
Outputs:
- mlp_out: bfloat16 [768, 6144], P(('groups', 'row'), 'col'), parts along dimension 0
There are 2 independent parts, one for each index of `groups`. A program takes and returns all parts, laid end to end along the dimension named above; an argument that names none is the same for every part. Nothing has to cross between parts.
Inputs may be any that keep to these rules, and one draw needn't show every extreme that they name: Activations with a spread of scales over tokens and features.
All inputs are finite; a program needn't handle non-finite values.
Results may differ from a plain program's by a relative error of at most 0.015.
Values may be sent and summed in bfloat16 or wider, within the bound.
A program may use at most 128 MiB of HBM per device.

v0:
```python
import jax
import jax.numpy as jnp
from jax import lax
from jax.sharding import PartitionSpec as P

D = 6144


def on_device(tokens, norm_gain, norm_bias, up_weight, up_bias, down_weight, down_bias):
    gathered = lax.all_gather(tokens, "row", axis=0, tiled=True)
    values = gathered.astype(jnp.float32)
    mean = lax.psum(jnp.sum(values, axis=1), "col") / D
    deviation = values - mean[:, None]
    variance = lax.psum(jnp.sum(deviation * deviation, axis=1), "col") / D
    normed = (deviation * lax.rsqrt(variance[:, None] + 1e-05) * norm_gain + norm_bias).astype(
        jnp.bfloat16
    )
    partial_value = jnp.dot(normed, up_weight, preferred_element_type=jnp.float32)
    pre = lax.psum(partial_value.astype(jnp.bfloat16), "col").astype(jnp.float32) + up_bias
    hidden = jax.nn.gelu(pre, approximate=True).astype(jnp.bfloat16)
    summed = lax.psum_scatter(
        jnp.dot(hidden, down_weight, preferred_element_type=jnp.float32).astype(jnp.bfloat16),
        "row",
        scatter_dimension=0,
        tiled=True,
    ).astype(jnp.float32)
    return (summed + down_bias).astype(jnp.bfloat16)


def solution(mesh):
    in_specs = (
        P(("groups", "row"), "col"),
        P("col"),
        P("col"),
        P("col", "row"),
        P("row"),
        P("row", "col"),
        P("col"),
    )
    out_specs = P(("groups", "row"), "col")
    return jax.shard_map(
        on_device, mesh=mesh, in_specs=in_specs, out_specs=out_specs, check_vma=False
    )
```

profile of v0, /device:TPU:0, one launch (start us, length us, event | category | flops | bytes accessed | tf_op | source)
XLA Modules:
  0.0 199.9 jit_solution(14507239134772979856)
XLA Ops:
  6.5 0.0 copy-start.2
  6.5 0.0 copy-start.3
  6.5 0.0 all-gather.2.cloned.1.call-start
  6.5 0.7 all-gather.2.cloned.1.call-update
  7.3 0.0 all-reduce.2.cloned.1.call-start
  7.3 57.0 %all-gather.2.cloned.1.call-done = bf16[384,3072]{1,0:T(8,128)(2,1)} async-done(((bf16[48,3072]{1,0:T(8,128)(2,1)}), bf16[384,3072]{1,0:T(8,128)(2,1)}) %all-gather.2.cloned.1.call-update) | async-done | bytes 2359312 | tf_op jit(solution)/shard_map/all_gather | solution.py:10
  64.4 0.0 copy-start
  64.4 2.2 %convert_reduce_fusion = f32[384]{0:T(512)S(1)} fusion(bf16[384,3072]{1,0:T(8,128)(2,1)} %all-gather.2.cloned.1.call-done), kind=kLoop, calls=%fused_computation.2 | loop fusion | flops 2358912 | bytes 2360832 | tf_op jit(solution)/shard_map/reduce_sum | solution.py:12
  66.6 2.5 %psum.21 = f32[384]{0:T(512)S(1)} all-reduce(f32[384]{0:T(512)S(1)} %convert_reduce_fusion), channel_id=1, replica_groups=mesh['groups'=2,'row'=8,'col'=2] {'col'}, use_global_device_ids=true, to_apply=%region_1.0 | all-reduce | flops 384 | bytes 3072 | tf_op jit(solution)/shard_map/psum | solution.py:12
  69.0 2.4 %fusion.2 = f32[384]{0:T(512)S(1)} fusion(bf16[384,3072]{1,0:T(8,128)(2,1)} %all-gather.2.cloned.1.call-done, f32[384]{0:T(512)S(1)} %broadcast_multiply_fusion), kind=kLoop, calls=%fused_computation.5 | loop fusion | flops 4718208 | bytes 2362368 | tf_op jit(solution)/shard_map/reduce_sum | solution.py:14
  71.4 2.5 %psum.22 = f32[384]{0:T(512)S(1)} all-reduce(f32[384]{0:T(512)S(1)} %fusion.2), channel_id=1, replica_groups=mesh['groups'=2,'row'=8,'col'=2] {'col'}, use_global_device_ids=true, to_apply=%region_3.0 | all-reduce | flops 384 | bytes 3072 | tf_op jit(solution)/shard_map/psum | solution.py:14
  73.9 0.0 copy-done.2
  73.9 0.0 copy-done.3
  73.9 0.0 copy-done
  73.9 0.0 copy-start.4
  74.0 12.8 %convolution_convert_fusion.1 = bf16[384,3072]{1,0:T(8,128)(2,1)} fusion(bf16[3072,3072]{1,0:T(8,128)(2,1)} %param.10, bf16[384,3072]{1,0:T(8,128)(2,1)S(1)} %copy-done, f32[3072]{0:T(1024)S(1)} %copy-done.2, f32[3072]{0:T(1024)S(1)} %copy-done.3, f32[384]{0:T(512)S(1)} %add_rsqrt_fusion, f32[384]{0:T(512)S(1)} %broadcast_multiply_fusion), kind=kOutput, calls=%fused_computation.18 | convolution fusion | flops 7256014848 | bytes 23620608 | tf_op jit(solution)/shard_map/dot_general | solution.py:18
  86.7 0.0 all-reduce.2.cloned.1.call-update
  86.8 0.0 copy-start.1
  86.8 0.0 reduce-scatter.2.cloned.1.call-start
  86.8 20.3 %all-reduce.2.cloned.1.call-done = bf16[384,3072]{1,0:T(8,128)(2,1)} async-done(((bf16[384,3072]{1,0:T(8,128)(2,1)}), bf16[384,3072]{1,0:T(8,128)(2,1)}) %all-reduce.2.cloned.1.call-update) | async-done | bytes 2359312 | tf_op jit(solution)/shard_map/psum | solution.py:19
  107.1 0.0 copy-done.4
  107.1 14.2 %convolution_convert_fusion = bf16[384,3072]{1,0:T(8,128)(2,1)} fusion(bf16[3072,3072]{1,0:T(8,128)(2,1)} %param.12, bf16[384,3072]{1,0:T(8,128)(2,1)} %all-reduce.2.cloned.1.call-done, f32[3072]{0:T(1024)S(1)} %copy-done.4), kind=kOutput, calls=%fused_computation.17 | convolution fusion | flops 7261913088 | bytes 23605248 | tf_op jit(solution)/shard_map/dot_general | solution.py:22
  121.2 0.0 reduce-scatter.2.cloned.1.call-update
  121.3 70.4 %reduce-scatter.2.cloned.1.call-done = bf16[48,3072]{1,0:T(8,128)(2,1)} async-done(((bf16[384,3072]{1,0:T(8,128)(2,1)}), bf16[48,3072]{1,0:T(8,128)(2,1)}) %reduce-scatter.2.cloned.1.call-update) | async-done | bytes 294928 | tf_op jit(solution)/shard_map/reduce_scatter | solution.py:21
  191.6 0.0 copy-done.1
  191.6 1.7 add_convert_fusion
  (2 shorter events, 0.0 us)
Async XLA Ops:
  6.5 67.4 %copy-start.2 = (f32[3072]{0:T(1024)S(1)}, f32[3072]{0:T(1024)}, u32[]{:S(2)}) copy-start(f32[3072]{0:T(1024)} %param.9) | copy-start | bytes 36868
  6.5 67.4 %copy-start.3 = (f32[3072]{0:T(1024)S(1)}, f32[3072]{0:T(1024)}, u32[]{:S(2)}) copy-start(f32[3072]{0:T(1024)} %param.8) | copy-start | bytes 36868
  6.5 57.8 %all-gather.2.cloned.1.call-start = ((), (), s32[]{:S(2)}) async-start(), calls=%async_computation.1 | async-start | bytes 2654208 | tf_op jit(solution)/shard_map/all_gather | solution.py:10
  7.3 99.8 %all-reduce.2.cloned.1.call-start = ((), (), s32[]{:S(2)}) async-start(), calls=%async_computation.2 | async-start | bytes 4718592 | tf_op jit(solution)/shard_map/psum | solution.py:19
  64.4 9.6 %copy-start = (bf16[384,3072]{1,0:T(8,128)(2,1)S(1)}, bf16[384,3072]{1,0:T(8,128)(2,1)}, u32[]{:S(2)}) copy-start(bf16[384,3072]{1,0:T(8,128)(2,1)} %all-gather.2.cloned.1.call-done) | copy-start | bytes 7077892
  73.9 33.1 %copy-start.4 = (f32[3072]{0:T(1024)S(1)}, f32[3072]{0:T(1024)}, u32[]{:S(2)}) copy-start(f32[3072]{0:T(1024)} %param.11) | copy-start | bytes 36868
  86.8 104.9 %copy-start.1 = (f32[3072]{0:T(1024)S(1)}, f32[3072]{0:T(1024)}, u32[]{:S(2)}) copy-start(f32[3072]{0:T(1024)} %param.13) | copy-start | bytes 36868
  86.8 104.9 %reduce-scatter.2.cloned.1.call-start = ((), (), s32[]{:S(2)}) async-start(), calls=%async_computation.3 | async-start | bytes 2654208 | tf_op jit(solution)/shard_map/reduce_scatter | solution.py:21
Sparse Core Ops, SparseCore 0:
  9.5 54.7 all-gather.1
  86.9 20.1 all-reduce.1
  121.4 70.1 reduce-scatter.1
where the time goes:
time: 200 us
  waiting for transfers between devices  148 us (74%)
  matrix products  26.9 us (13%)
  between operations  13.1 us (7%)
  other arithmetic  6.36 us (3%)
  blocking collectives  4.93 us (2%)
    reduce_scatter x1, waiting for transfers between devices, on_device(): lax.psum_scatter(jnp.dot(hidden, down_weight, preferred_element_type=jnp....  70.4 us
    all_gather x1, waiting for transfers between devices, on_device(): gathered = lax.all_gather(tokens, 'row', axis=0, tiled=True)  57 us
    psum x1, waiting for transfers between devices, on_device(): lax.psum(partial_value.astype(jnp.bfloat16), 'col').astype(jnp.float32)  20.3 us
    dot_general x1, matrix products, on_device(): jnp.dot(hidden, down_weight, preferred_element_type=jnp.float32)  14.2 us
    dot_general x1, matrix products, on_device(): jnp.dot(normed, up_weight, preferred_element_type=jnp.float32)  12.8 us
  transfers between devices with their start and end apart: 3, of which 3 were waited for; matrix products, arithmetic and copies ran while one was open for 0% of the time, Pallas kernels for 0%

commit v1 on v0

v1 whole, which is shorter than its diff:
```python
import functools

import jax
import jax.numpy as jnp
from jax import lax
from jax.experimental import pallas as pl
from jax.experimental.pallas import tpu as pltpu
from jax.sharding import PartitionSpec as P

MESH = pl.DeviceIdType.MESH
F32 = jnp.float32
BF16 = jnp.bfloat16


def kernel(
    nz, ny,
    tok_ref, gain_ref, nbias_ref, w1_hbm, ubias_ref, w2_hbm, dbias_ref, out_ref,
    w1, w2, x_all, ppart, psend, precv, hidden, pout, yrecv, zrecv, stat, stat_in,
    w_sem, st_sem, x_recv, x_up, x_dn, x_y, p_s, p_r, y_s, y_r, z_s, z_r,
):
    r = lax.axis_index("row")
    c = lax.axis_index("col")
    z, y = r // ny, r % ny
    t, dh = tok_ref.shape
    ff = w1.shape[1]
    rows = ny * t
    wide = 512 if ff % 512 == 0 else 256
    core = {"col": 1 - c}

    def row_of(level, column):
        return level * ny + column

    def remote(src, dst, s_sem, r_sem, device):
        return pltpu.make_async_remote_copy(
            src_ref=src, dst_ref=dst, send_sem=s_sem, recv_sem=r_sem,
            device_id=device, device_id_type=MESH,
        )

    load1 = pltpu.make_async_copy(w1_hbm, w1, w_sem.at[0])
    load2 = pltpu.make_async_copy(w2_hbm, w2, w_sem.at[1])
    load1.start()
    load2.start()

    x = tok_ref[...].astype(F32)
    mean_here = jnp.sum(x, axis=1, keepdims=True) / dh
    dev = x - mean_here
    m2_here = jnp.sum(dev * dev, axis=1, keepdims=True)
    stat[0] = jnp.broadcast_to(mean_here, (t, 128))
    stat[1] = jnp.broadcast_to(m2_here, (t, 128))

    barrier = pltpu.get_barrier_semaphore()
    pl.semaphore_signal(barrier, inc=1, device_id=core, device_id_type=MESH)
    if ny == 2:
        pl.semaphore_signal(
            barrier, inc=1, device_id={"row": row_of(z, 1 - y)}, device_id_type=MESH
        )

    @pl.when(z > 0)
    def _():
        pl.semaphore_signal(
            barrier, inc=1, device_id={"row": row_of(z - 1, y)}, device_id_type=MESH
        )

    @pl.when(z < nz - 1)
    def _():
        pl.semaphore_signal(
            barrier, inc=1, device_id={"row": row_of(z + 1, y)}, device_id_type=MESH
        )

    pl.semaphore_wait(barrier, ny + jnp.where(z > 0, 1, 0) + jnp.where(z < nz - 1, 1, 0))

    swap = remote(stat, stat_in, st_sem.at[0], st_sem.at[1], core)
    swap.start()
    swap.wait()
    other_mean = stat_in[0][:, :1]
    other_m2 = stat_in[1][:, :1]
    gap = mean_here - other_mean
    mean = 0.5 * (mean_here + other_mean)
    var = (m2_here + other_m2 + (0.5 * dh) * gap * gap) / (2 * dh)
    x_all[r] = (
        (tok_ref[...].astype(F32) - mean) * lax.rsqrt(var + 1e-05) * gain_ref[...] + nbias_ref[...]
    ).astype(BF16)

    def x_copy(level, sems, device_row):
        slot = row_of(level, y)
        return remote(
            x_all.at[slot], x_all.at[slot], sems.at[level], x_recv.at[slot], {"row": device_row}
        )

    def up_copy(level):
        return x_copy(level, x_up, row_of(z + 1, y))

    def dn_copy(level):
        return x_copy(level, x_dn, row_of(z - 1, y))

    def y_copy(level):
        return x_copy(level, x_y, row_of(z, 1 - y))

    def x_wait(slot):
        remote(
            x_all.at[slot], x_all.at[slot], x_up.at[0], x_recv.at[slot], core
        ).wait_recv()

    def p_copy(level):
        return remote(psend.at[level], precv.at[level], p_s.at[level], p_r.at[level], core)

    def process(level):
        if ny == 2:
            x_wait(row_of(level, 1 - y))

        @pl.loop(0, ff // wide)
        def _(j):
            cols = pl.ds(pl.multiple_of(j * wide, wide), wide)
            block = x_all[pl.ds(level * ny, ny)].reshape(rows, dh)
            value = jnp.dot(block, w1[:, cols], preferred_element_type=F32)
            ppart[level, :, cols] = value
            psend[level, :, cols] = value.astype(BF16)

        p_copy(level).start()

    def finish(level):
        p_copy(level).wait_recv()

        @pl.loop(0, ff // wide)
        def _(j):
            cols = pl.ds(pl.multiple_of(j * wide, wide), wide)
            pre = ppart[level, :, cols] + precv[level, :, cols].astype(F32) + ubias_ref[:, cols]
            hidden[level, :, cols] = jax.nn.gelu(pre, approximate=True).astype(BF16)

    def each_at(d, act):
        @pl.when((d >= 0) & (z - d >= 0))
        def _():
            act(z - d)

        @pl.when((d > 0) & (z + d <= nz - 1))
        def _():
            act(z + d)

    @pl.loop(0, nz + 2)
    def _(s):
        @pl.when((s > 0) & (z - s >= 0))
        def _():
            x_wait(row_of(z - s, y))

        @pl.when((s < nz) & (z - s >= 0) & (z < nz - 1))
        def _():
            up_copy(z - s).start()

        if ny == 2:
            @pl.when((s < nz) & (z - s >= 0))
            def _():
                y_copy(z - s).start()

        @pl.when((s > 0) & (z + s <= nz - 1))
        def _():
            x_wait(row_of(z + s, y))

        @pl.when((s < nz) & (z + s <= nz - 1) & (z > 0))
        def _():
            dn_copy(z + s).start()

        if ny == 2:
            @pl.when((s > 0) & (z + s <= nz - 1))
            def _():
                y_copy(z + s).start()

        @pl.when(s == 1)
        def _():
            load1.wait()

        each_at(s - 1, process)
        each_at(s - 2, finish)

    load2.wait()

    def yp_copy(level):
        return remote(
            pout.at[row_of(level, 1 - y)], yrecv.at[level], y_s.at[level], y_r.at[level],
            {"row": row_of(z, 1 - y)},
        )

    def project(level):
        @pl.loop(0, dh // wide)
        def _(j):
            cols = pl.ds(pl.multiple_of(j * wide, wide), wide)
            value = jnp.dot(hidden[level], w2[:, cols], preferred_element_type=F32)
            pout[pl.ds(level * ny, ny), :, cols] = value.astype(BF16).reshape(ny, t, wide)

        if ny == 2:
            yp_copy(level).start()

    def zd_copy(level):
        slot = jnp.where(z - 1 == level, nz, level)
        return remote(
            pout.at[row_of(level, y)], zrecv.at[slot], z_s.at[level], z_r.at[slot],
            {"row": row_of(z - 1, y)},
        )

    def zu_copy(level):
        return remote(
            pout.at[row_of(level, y)], zrecv.at[level], z_s.at[level], z_r.at[level],
            {"row": row_of(z + 1, y)},
        )

    def z_wait(slot):
        remote(
            zrecv.at[slot], zrecv.at[slot], z_s.at[0], z_r.at[slot], core
        ).wait_recv()

    def reduce(level):
        slot = row_of(level, y)
        inner = ((level < z) & (z < nz - 1)) | ((level > z) & (z > 0))
        if ny == 2:
            yp_copy(level).wait_recv()

        @pl.when(inner)
        def _():
            z_wait(level)
            total = pout[slot].astype(F32) + zrecv[level].astype(F32)
            if ny == 2:
                total += yrecv[level].astype(F32)
            pout[slot] = total.astype(BF16)

        if ny == 2:
            @pl.when(jnp.logical_not(inner))
            def _():
                pout[slot] = (pout[slot].astype(F32) + yrecv[level].astype(F32)).astype(BF16)

        @pl.when(level < z)
        def _():
            zd_copy(level).start()

        @pl.when(level > z)
        def _():
            zu_copy(level).start()

    @pl.loop(0, nz)
    def _(s):
        d = nz - 1 - s
        each_at(d, project)

        @pl.when(d < nz - 1)
        def _():
            each_at(d + 1, reduce)

    if ny == 2:
        yp_copy(z).wait_recv()
    total = pout[r].astype(F32)
    if ny == 2:
        total += yrecv[z].astype(F32)
    lower = (z > 0)
    upper = (z < nz - 1)

    ppart_own = total + dbias_ref[...]

    @pl.when(lower & upper)
    def _():
        z_wait(z)
        z_wait(nz)
        out_ref[...] = (ppart_own + zrecv[z].astype(F32) + zrecv[nz].astype(F32)).astype(BF16)

    @pl.when(lower & jnp.logical_not(upper))
    def _():
        z_wait(z)
        out_ref[...] = (ppart_own + zrecv[z].astype(F32)).astype(BF16)

    @pl.when(upper & jnp.logical_not(lower))
    def _():
        z_wait(nz)
        out_ref[...] = (ppart_own + zrecv[nz].astype(F32)).astype(BF16)

    @pl.loop(0, nz)
    def _(level):
        @pl.when((level <= z) & (z < nz - 1))
        def _():
            up_copy(level).wait_send()

        @pl.when((level >= z) & (z > 0))
        def _():
            dn_copy(level).wait_send()

        if ny == 2:
            y_copy(level).wait_send()
            yp_copy(level).wait_send()
        p_copy(level).wait_send()

        @pl.when(level != z)
        def _():
            zu_copy(level).wait_send()


def solution(mesh):
    n_row = mesh.shape["row"]
    ny = 2 if n_row == 8 else 1
    nz = n_row // ny

    def on_device(tokens, norm_gain, norm_bias, up_weight, up_bias, down_weight, down_bias):
        t, dh = tokens.shape
        ff = up_weight.shape[1]
        dout = down_weight.shape[1]
        vmem = pl.BlockSpec(memory_space=pltpu.VMEM)
        hbm = pl.BlockSpec(memory_space=pl.ANY)
        dma = pltpu.SemaphoreType.DMA
        rows = ny * t
        return pl.pallas_call(
            functools.partial(kernel, nz, ny),
            out_shape=jax.ShapeDtypeStruct((t, dout), BF16),
            in_specs=[vmem, vmem, vmem, hbm, vmem, hbm, vmem],
            out_specs=vmem,
            scratch_shapes=[
                pltpu.VMEM((dh, ff), BF16),
                pltpu.VMEM((ff, dout), BF16),
                pltpu.VMEM((n_row, t, dh), BF16),
                pltpu.VMEM((nz, rows, ff), F32),
                pltpu.VMEM((nz, rows, ff), BF16),
                pltpu.VMEM((nz, rows, ff), BF16),
                pltpu.VMEM((nz, rows, ff), BF16),
                pltpu.VMEM((n_row, t, dout), BF16),
                pltpu.VMEM((nz if ny == 2 else 1, t, dout), BF16),
                pltpu.VMEM((nz + 1, t, dout), BF16),
                pltpu.VMEM((2, t, 128), F32),
                pltpu.VMEM((2, t, 128), F32),
                dma((2,)), dma((2,)), dma((n_row,)),
                dma((nz,)), dma((nz,)), dma((nz,)),
                dma((nz,)), dma((nz,)), dma((nz,)), dma((nz,)),
                dma((nz,)), dma((nz + 1,)),
            ],
            compiler_params=pltpu.CompilerParams(
                collective_id=0, has_side_effects=True, vmem_limit_bytes=62 * 1024 * 1024
            ),
            cost_estimate=pl.CostEstimate(
                flops=4 * n_row * t * dh * ff, bytes_accessed=4 * dh * ff, transcendentals=0
            ),
        )(
            tokens, norm_gain.reshape(1, -1), norm_bias.reshape(1, -1), up_weight,
            up_bias.reshape(1, -1), down_weight, down_bias.reshape(1, -1),
        )

    in_specs = (
        P(("groups", "row"), "col"),
        P("col"),
        P("col"),
        P("col", "row"),
        P("row"),
        P("row", "col"),
        P("col"),
    )
    out_specs = P(("groups", "row"), "col")
    return jax.shard_map(
        on_device, mesh=mesh, in_specs=in_specs, out_specs=out_specs, check_vma=False
    )
```

time: 200 us -> 82 us (0.41)
  waiting for transfers between devices: 148 us -> 0 us
  Pallas kernels: 0 us -> 80.2 us
  matrix products: 26.9 us -> 0 us
  between operations: 13.1 us -> 0.01 us
  other arithmetic: 6.36 us -> 0 us
  blocking collectives: 4.93 us -> 0 us
    pallas_call x0 -> x1, Pallas kernels: none -> 80.2 us  [on_device(): pl.pallas_call(functools.partial(kernel, nz, ny), out_shape=jax.ShapeDtyp...]
    reduce_scatter x1 -> x0, waiting for transfers between devices: 70.4 us -> none  [on_device(): lax.psum_scatter(jnp.dot(hidden, down_weight, preferred_element_type=jnp....]
    all_gather x1 -> x0, waiting for transfers between devices: 57 us -> none  [on_device(): gathered = lax.all_gather(tokens, 'row', axis=0, tiled=True)]
    dot_general x2 -> x0, matrix products: 26.9 us -> none  [the longest x1 14.2 us: on_device(): jnp.dot(hidden, down_weight, preferred_element_type=jnp.float32)]
    psum x1 -> x0, waiting for transfers between devices: 20.3 us -> none  [on_device(): lax.psum(partial_value.astype(jnp.bfloat16), 'col').astype(jnp.float32)]
    psum x2 -> x0, blocking collectives: 4.93 us -> none  [the longest x1 2.47 us: on_device(): variance = lax.psum(jnp.sum(deviation * deviation, axis=1), 'col') / D]
    reduce_sum x2 -> x0, other arithmetic: 4.62 us -> none  [the longest x1 2.42 us: on_device(): variance = lax.psum(jnp.sum(deviation * deviation, axis=1), 'col') / D]
  transfers between devices with their start and end apart: 3 -> 0, of which waited for: 3 -> 0; matrix products, arithmetic and copies ran while one was open for 0% -> 0% of each run, Pallas kernels for 0% -> 0%
where the time goes in v1:
time: 82 us; the launch traced here: 81.9 us
  Pallas kernels  80.2 us (98%)
  local copies, waits for them, and re-layouts  1.69 us (2%)
    pallas_call x1, Pallas kernels, on_device(): pl.pallas_call(functools.partial(kernel, nz, ny), out_shape=jax.ShapeDtyp...  80.2 us
    unnamed x1, local copies, waits for them, and re-layouts  1.69 us

profile of v1, /device:TPU:0, one launch (start us, length us, event | category | flops | bytes accessed | tf_op | source)
XLA Modules:
  0.0 81.9 jit_solution(1193627296013770794)
XLA Ops:
  0.0 80.2 %shard_map.73 = bf16[48,3072]{1,0:T(8,128)(2,1)} custom-call(bf16[48,3072]{1,0:T(8,128)(2,1)} %tok_ref.1, f32[1,3072]{1,0:T(1,128)} %bitcast.4, f32[1,3072]{1,0:T(1,128)} %bitcast.5, bf16[3072,3072]{1,0:T(8,128)(2,1)} %w1_hbm.1, f32[1,3072]{1,0:T(1,128)} %bitcast.6, bf16[3072,3072]{1,0:T(8,128)(2,1)} %w2_hbm.1, f32[1,3072]{1,0:T(1,128)} %bitcast.7), custom_call_target="tpu_custom_call" | custom-call | flops 14495514624 | bytes 37748736 | tf_op jit(solution)/shard_map/pallas_call | solution.py:305
  80.2 1.7 %copy.9 = bf16[48,3072]{1,0:T(8,128)(2,1)} copy(bf16[48,3072]{1,0:T(8,128)(2,1)} %shard_map.73) | data formatting | bytes 589824

commit v2 on v1

v2 whole, which is shorter than its diff:
```python
import functools

import jax
import jax.numpy as jnp
from jax import lax
from jax.experimental import pallas as pl
from jax.experimental.pallas import tpu as pltpu
from jax.sharding import PartitionSpec as P

MESH = pl.DeviceIdType.MESH
F32 = jnp.float32
BF16 = jnp.bfloat16


def kernel(
    nz, ny,
    tok_ref, gain_ref, nbias_ref, w1_hbm, ubias_ref, w2_hbm, dbias_ref, out_ref,
    w1, w2, x_all, ppart, psend, precv, hidden, pout, yrecv, zrecv, zside, acc, stat, stat_in,
    w_sem, st_sem, x_recv, x_up, x_dn, x_y, p_s, p_r, y_s, y_r, z_s, z_r,
):
    r = lax.axis_index("row")
    c = lax.axis_index("col")
    z, y = r // ny, r % ny
    t, dh = tok_ref.shape
    ff = w1.shape[1]
    rows = ny * t
    wide = 1024 if ff % 1024 == 0 else 256
    core = {"col": 1 - c}

    def row_of(level, column):
        return level * ny + column

    def remote(src, dst, s_sem, r_sem, device):
        return pltpu.make_async_remote_copy(
            src_ref=src, dst_ref=dst, send_sem=s_sem, recv_sem=r_sem,
            device_id=device, device_id_type=MESH,
        )

    load1 = pltpu.make_async_copy(w1_hbm, w1, w_sem.at[0])
    load2 = pltpu.make_async_copy(w2_hbm, w2, w_sem.at[1])
    load1.start()
    load2.start()

    x = tok_ref[...].astype(F32)
    mean_here = jnp.sum(x, axis=1, keepdims=True) / dh
    dev = x - mean_here
    m2_here = jnp.sum(dev * dev, axis=1, keepdims=True)
    stat[0] = jnp.broadcast_to(mean_here, (t, 128))
    stat[1] = jnp.broadcast_to(m2_here, (t, 128))

    barrier = pltpu.get_barrier_semaphore()
    pl.semaphore_signal(barrier, inc=1, device_id=core, device_id_type=MESH)
    if ny == 2:
        pl.semaphore_signal(
            barrier, inc=1, device_id={"row": row_of(z, 1 - y)}, device_id_type=MESH
        )

    @pl.when(z > 0)
    def _():
        pl.semaphore_signal(
            barrier, inc=1, device_id={"row": row_of(z - 1, y)}, device_id_type=MESH
        )

    @pl.when(z < nz - 1)
    def _():
        pl.semaphore_signal(
            barrier, inc=1, device_id={"row": row_of(z + 1, y)}, device_id_type=MESH
        )

    pl.semaphore_wait(barrier, ny + jnp.where(z > 0, 1, 0) + jnp.where(z < nz - 1, 1, 0))

    swap = remote(stat, stat_in, st_sem.at[0], st_sem.at[1], core)
    swap.start()
    swap.wait()
    other_mean = stat_in[0][:, :1]
    other_m2 = stat_in[1][:, :1]
    gap = mean_here - other_mean
    mean = 0.5 * (mean_here + other_mean)
    var = (m2_here + other_m2 + (0.5 * dh) * gap * gap) / (2 * dh)
    x_all[r] = (
        (tok_ref[...].astype(F32) - mean) * lax.rsqrt(var + 1e-05) * gain_ref[...] + nbias_ref[...]
    ).astype(BF16)

    edges = (0, dh // 6, dh // 2, dh)
    cut = [pl.ds(edges[k], edges[k + 1] - edges[k]) for k in range(3)]
    plain = (1, 2) if ny == 2 else (1, 2, 0)

    def x_copy(slot, k, sems, device_row):
        part = x_all.at[slot, :, cut[k]]
        return remote(part, part, sems.at[slot, k], x_recv.at[slot, k], {"row": device_row})

    def up_copy(slot, k):
        return x_copy(slot, k, x_up, row_of(z + 1, y))

    def dn_copy(slot, k):
        return x_copy(slot, k, x_dn, row_of(z - 1, y))

    def y_copy(slot, k):
        return x_copy(slot, k, x_y, row_of(z, 1 - y))

    def x_wait(slot, k):
        x_copy(slot, k, x_up, r).wait_recv()

    def p_copy(level):
        return remote(psend.at[level], precv.at[level], p_s.at[level], p_r.at[level], core)

    def process(level):
        if ny == 2:
            for k in plain:
                x_wait(row_of(level, 1 - y), k)

        @pl.loop(0, ff // wide)
        def _(j):
            cols = pl.ds(pl.multiple_of(j * wide, wide), wide)
            block = x_all[pl.ds(level * ny, ny)].reshape(rows, dh)
            value = jnp.dot(block, w1[:, cols], preferred_element_type=F32)
            ppart[level, :, cols] = value
            psend[level, :, cols] = value.astype(BF16)

        p_copy(level).start()

    def finish(level):
        p_copy(level).wait_recv()

        @pl.loop(0, ff // wide)
        def _(j):
            cols = pl.ds(pl.multiple_of(j * wide, wide), wide)
            pre = ppart[level, :, cols] + precv[level, :, cols].astype(F32) + ubias_ref[:, cols]
            hidden[level, :, cols] = jax.nn.gelu(pre, approximate=True).astype(BF16)

    def yp_copy(level, k):
        return remote(
            pout.at[row_of(level, 1 - y), :, cut[k]], yrecv.at[level, :, cut[k]],
            y_s.at[level, k], y_r.at[level, k], {"row": row_of(z, 1 - y)},
        )

    def send_y(level):
        if ny == 2:
            for k in plain:
                yp_copy(level, k).start()

    def project(level):
        step = 512 if edges[1] % 512 == 0 else 128
        for k in (1, 2, 0):
            @pl.loop(edges[k] // step, edges[k + 1] // step)
            def _(j):
                cols = pl.ds(pl.multiple_of(j * step, step), step)
                value = jnp.dot(hidden[level], w2[:, cols], preferred_element_type=F32)
                pout[pl.ds(level * ny, ny), :, cols] = value.astype(BF16).reshape(ny, t, step)

            if ny == 2 and k in plain:
                @pl.when(is_far(level))
                def _():
                    yp_copy(level, k).start()

    def is_far(level):
        return (z - level >= nz - 2) | (level - z >= nz - 2)

    def each_at(d, act):
        @pl.when((d >= 0) & (z - d >= 0))
        def _():
            act(z - d)

        @pl.when((d > 0) & (z + d <= nz - 1))
        def _():
            act(z + d)

    below_ok = z > 0
    above_ok = z < nz - 1

    if ny == 2:
        y_copy(r, 0).start()
    for k in (1, 2, 0):
        @pl.when(above_ok)
        def _():
            up_copy(r, k).start()

        @pl.when(below_ok)
        def _():
            dn_copy(r, k).start()

        if ny == 2 and k in plain:
            y_copy(r, k).start()
    if ny == 2:
        mate = row_of(z, 1 - y)
        x_wait(mate, 0)

        @pl.when(above_ok)
        def _():
            up_copy(mate, 0).start()

        @pl.when(below_ok)
        def _():
            dn_copy(mate, 0).start()

    def relay(s, column, k, cross):
        @pl.when(z - s >= 0)
        def _():
            slot = row_of(z - s, column)
            x_wait(slot, k)

            @pl.when(above_ok)
            def _():
                up_copy(slot, k).start()

            if cross:
                y_copy(slot, k).start()

        @pl.when(z + s <= nz - 1)
        def _():
            slot = row_of(z + s, column)
            x_wait(slot, k)

            @pl.when(below_ok)
            def _():
                dn_copy(slot, k).start()

            if cross:
                y_copy(slot, k).start()

    load1.wait()

    @pl.loop(1, nz + 1)
    def _(s):
        @pl.when(s < nz)
        def _():
            for k in plain:
                relay(s, y, k, ny == 2)
            if ny == 2:
                relay(s, y, 0, False)
                relay(s, 1 - y, 0, False)

        each_at(s - 1, process)

        @pl.when(s == 1)
        def _():
            load2.wait()

        each_at(s - 1, finish)
        each_at(s - 1, project)

    @pl.loop(0, nz)
    def _(i):
        def late(level):
            @pl.when(jnp.logical_not(is_far(level)))
            def _():
                send_y(level)

        each_at(nz - 1 - i, late)

    def zd_copy(level, k):
        slot = jnp.where(z - 1 == level, nz, level)
        return z_copy(level, slot, k, row_of(z - 1, y))

    def zu_copy(level, k):
        return z_copy(level, level, k, row_of(z + 1, y))

    def z_copy(level, slot, k, device_row):
        if k == 3:
            src, dst = pout.at[row_of(level, 1 - y), :, cut[0]], zside.at[slot]
        else:
            src, dst = pout.at[row_of(level, y), :, cut[k]], zrecv.at[slot, :, cut[k]]
        return remote(src, dst, z_s.at[level, k], z_r.at[slot, k], {"row": device_row})

    def z_wait(slot, k):
        level = jnp.where(slot == nz, 0, slot)
        z_copy(level, slot, k, r).wait_recv()

    def incoming(slot, k):
        return zside[slot] if k == 3 else zrecv[slot, :, cut[k]]

    def reduce(level):
        inner = ((level < z) & above_ok) | ((level > z) & below_ok)
        order = (0, 3, 1, 2) if ny == 2 else plain
        for k in order:
            slot = row_of(level, 1 - y if k == 3 else y)
            where = cut[0] if k == 3 else cut[k]
            crossed = ny == 2 and k in plain
            if crossed:
                yp_copy(level, k).wait_recv()

            @pl.when(inner)
            def _():
                z_wait(level, k)
                total = pout[slot, :, where].astype(F32) + incoming(level, k).astype(F32)
                if crossed:
                    total += yrecv[level, :, where].astype(F32)
                pout[slot, :, where] = total.astype(BF16)

            if crossed:
                @pl.when(jnp.logical_not(inner))
                def _():
                    pout[slot, :, where] = (
                        pout[slot, :, where].astype(F32) + yrecv[level, :, where].astype(F32)
                    ).astype(BF16)

            @pl.when(level < z)
            def _():
                zd_copy(level, k).start()

            @pl.when(level > z)
            def _():
                zu_copy(level, k).start()

    @pl.loop(0, nz - 1)
    def _(i):
        each_at(nz - 1 - i, reduce)

    def settle(k):
        slot = row_of(z, 1 - y) if k == 3 else r
        where = cut[0] if k == 3 else cut[k]
        acc[:, where] = pout[slot, :, where].astype(F32)

        @pl.when(below_ok)
        def _():
            z_wait(z, k)
            acc[:, where] += incoming(z, k).astype(F32)

        @pl.when(above_ok)
        def _():
            z_wait(nz, k)
            acc[:, where] += incoming(nz, k).astype(F32)

    if ny == 2:
        settle(3)
        pout[row_of(z, 1 - y), :, cut[0]] = acc[:, cut[0]].astype(BF16)
        yp_copy(z, 0).start()
    for k in (1, 2, 0):
        settle(k)
        total = acc[:, cut[k]] + dbias_ref[:, cut[k]]
        if ny == 2:
            yp_copy(z, k).wait_recv()
            total += yrecv[z, :, cut[k]].astype(F32)
        out_ref[:, cut[k]] = total.astype(BF16)

    @pl.loop(0, nz)
    def _(level):
        slots = [(row_of(level, y), k) for k in range(3)]
        if ny == 2:
            slots.append((row_of(level, 1 - y), 0))

        @pl.when((level <= z) & above_ok)
        def _():
            for slot, k in slots:
                up_copy(slot, k).wait_send()

        @pl.when((level >= z) & below_ok)
        def _():
            for slot, k in slots:
                dn_copy(slot, k).wait_send()

        if ny == 2:
            for k in plain:
                y_copy(row_of(level, y), k).wait_send()
                yp_copy(level, k).wait_send()
        p_copy(level).wait_send()

        @pl.when(level != z)
        def _():
            for k in range(4 if ny == 2 else 3):
                zu_copy(level, k).wait_send()

    if ny == 2:
        y_copy(r, 0).wait_send()
        yp_copy(z, 0).wait_send()


def solution(mesh):
    n_row = mesh.shape["row"]
    ny = 2 if n_row == 8 else 1
    nz = n_row // ny

    def on_device(tokens, norm_gain, norm_bias, up_weight, up_bias, down_weight, down_bias):
        t, dh = tokens.shape
        ff = up_weight.shape[1]
        dout = down_weight.shape[1]
        vmem = pl.BlockSpec(memory_space=pltpu.VMEM)
        hbm = pl.BlockSpec(memory_space=pl.ANY)
        dma = pltpu.SemaphoreType.DMA
        rows = ny * t
        return pl.pallas_call(
            functools.partial(kernel, nz, ny),
            out_shape=jax.ShapeDtypeStruct((t, dout), BF16),
            in_specs=[vmem, vmem, vmem, hbm, vmem, hbm, vmem],
            out_specs=vmem,
            scratch_shapes=[
                pltpu.VMEM((dh, ff), BF16),
                pltpu.VMEM((ff, dout), BF16),
                pltpu.VMEM((n_row, t, dh), BF16),
                pltpu.VMEM((nz, rows, ff), F32),
                pltpu.VMEM((nz, rows, ff), BF16),
                pltpu.VMEM((nz, rows, ff), BF16),
                pltpu.VMEM((nz, rows, ff), BF16),
                pltpu.VMEM((n_row, t, dout), BF16),
                pltpu.VMEM((nz if ny == 2 else 1, t, dout), BF16),
                pltpu.VMEM((nz + 1, t, dout), BF16),
                pltpu.VMEM((nz + 1 if ny == 2 else 1, t, dout // 6), BF16),
                pltpu.VMEM((t, dout), F32),
                pltpu.VMEM((2, t, 128), F32),
                pltpu.VMEM((2, t, 128), F32),
                dma((2,)), dma((2,)), dma((n_row, 3)),
                dma((n_row, 3)), dma((n_row, 3)), dma((n_row, 3)),
                dma((nz,)), dma((nz,)), dma((nz, 3)), dma((nz, 3)),
                dma((nz, 4)), dma((nz + 1, 4)),
            ],
            compiler_params=pltpu.CompilerParams(
                collective_id=0, has_side_effects=True, vmem_limit_bytes=62 * 1024 * 1024
            ),
            cost_estimate=pl.CostEstimate(
                flops=4 * n_row * t * dh * ff, bytes_accessed=4 * dh * ff, transcendentals=0
            ),
        )(
            tokens, norm_gain.reshape(1, -1), norm_bias.reshape(1, -1), up_weight,
            up_bias.reshape(1, -1), down_weight, down_bias.reshape(1, -1),
        )

    in_specs = (
        P(("groups", "row"), "col"),
        P("col"),
        P("col"),
        P("col", "row"),
        P("row"),
        P("row", "col"),
        P("col"),
    )
    out_specs = P(("groups", "row"), "col")
    return jax.shard_map(
        on_device, mesh=mesh, in_specs=in_specs, out_specs=out_specs, check_vma=False
    )
```

time: 82 us -> 81 us (0.988)
  Pallas kernels: 80.2 us -> 79 us
    pallas_call x1, Pallas kernels: 80.2 us -> 79 us  [on_device(): pl.pallas_call(functools.partial(kernel, nz, ny), out_shape=jax.ShapeDtyp...]
where the time goes in v2:
time: 81 us; the launch traced here: 80.7 us
  Pallas kernels  79 us (98%)
  local copies, waits for them, and re-layouts  1.69 us (2%)
    pallas_call x1, Pallas kernels, on_device(): pl.pallas_call(functools.partial(kernel, nz, ny), out_shape=jax.ShapeDtyp...  79 us
    unnamed x1, local copies, waits for them, and re-layouts  1.69 us

profile of v2, /device:TPU:0, one launch (start us, length us, event | category | flops | bytes accessed | tf_op | source)
XLA Modules:
  0.0 80.7 jit_solution(18176223403105332766)
XLA Ops:
  0.0 79.0 %shard_map.73 = bf16[48,3072]{1,0:T(8,128)(2,1)} custom-call(bf16[48,3072]{1,0:T(8,128)(2,1)} %tok_ref.1, f32[1,3072]{1,0:T(1,128)} %bitcast.4, f32[1,3072]{1,0:T(1,128)} %bitcast.5, bf16[3072,3072]{1,0:T(8,128)(2,1)} %w1_hbm.1, f32[1,3072]{1,0:T(1,128)} %bitcast.6, bf16[3072,3072]{1,0:T(8,128)(2,1)} %w2_hbm.1, f32[1,3072]{1,0:T(1,128)} %bitcast.7), custom_call_target="tpu_custom_call" | custom-call | flops 14495514624 | bytes 37748736 | tf_op jit(solution)/shard_map/pallas_call | solution.py:381
  79.0 1.7 %copy.9 = bf16[48,3072]{1,0:T(8,128)(2,1)} copy(bf16[48,3072]{1,0:T(8,128)(2,1)} %shard_map.73) | data formatting | bytes 589824

commit v3 on v2

--- a/solution.py
+++ b/solution.py
@@ -24,7 +24,7 @@
     t, dh = tok_ref.shape
     ff = w1.shape[1]
     rows = ny * t
-    wide = 1024 if ff % 1024 == 0 else 256
+    wide = ff
     core = {"col": 1 - c}
 
     def row_of(level, column):
@@ -134,27 +134,17 @@
             y_s.at[level, k], y_r.at[level, k], {"row": row_of(z, 1 - y)},
         )
 
-    def send_y(level):
-        if ny == 2:
-            for k in plain:
-                yp_copy(level, k).start()
-
     def project(level):
         step = 512 if edges[1] % 512 == 0 else 128
         for k in (1, 2, 0):
-            @pl.loop(edges[k] // step, edges[k + 1] // step)
-            def _(j):
-                cols = pl.ds(pl.multiple_of(j * step, step), step)
+            if True:
+                step = edges[k + 1] - edges[k]
+                cols = cut[k]
                 value = jnp.dot(hidden[level], w2[:, cols], preferred_element_type=F32)
                 pout[pl.ds(level * ny, ny), :, cols] = value.astype(BF16).reshape(ny, t, step)
 
             if ny == 2 and k in plain:
-                @pl.when(is_far(level))
-                def _():
-                    yp_copy(level, k).start()
-
-    def is_far(level):
-        return (z - level >= nz - 2) | (level - z >= nz - 2)
+                yp_copy(level, k).start()
 
     def each_at(d, act):
         @pl.when((d >= 0) & (z - d >= 0))
@@ -232,21 +222,18 @@
 
         each_at(s - 1, process)
 
-        @pl.when(s == 1)
+        @pl.when(s - 2 < nz - 2)
+        def _():
+            each_at(s - 2, finish)
+
+        @pl.when(s - 1 == nz - 2)
         def _():
             load2.wait()
 
-        each_at(s - 1, finish)
-        each_at(s - 1, project)
-
-    @pl.loop(0, nz)
-    def _(i):
-        def late(level):
-            @pl.when(jnp.logical_not(is_far(level)))
-            def _():
-                send_y(level)
-
-        each_at(nz - 1 - i, late)
+        @pl.when(s - 1 >= nz - 2)
+        def _():
+            each_at(s - 1, finish)
+            each_at(s - 1, project)
 
     def zd_copy(level, k):
         slot = jnp.where(z - 1 == level, nz, level)
@@ -304,6 +291,7 @@
 
     @pl.loop(0, nz - 1)
     def _(i):
+        each_at(nz - 3 - i, project)
         each_at(nz - 1 - i, reduce)
 
     def settle(k):

time: 81 us -> 78.7 us (0.972)
  Pallas kernels: 79 us -> 75.9 us
    pallas_call x1, Pallas kernels: 79 us -> 75.9 us  [on_device(): pl.pallas_call(functools.partial(kernel, nz, ny), out_shape=jax.ShapeDtyp...]
where the time goes in v3:
time: 78.7 us; the launch traced here: 77.6 us
  Pallas kernels  75.9 us (96%)
  local copies, waits for them, and re-layouts  1.69 us (2%)
    pallas_call x1, Pallas kernels, on_device(): pl.pallas_call(functools.partial(kernel, nz, ny), out_shape=jax.ShapeDtyp...  75.9 us
    unnamed x1, local copies, waits for them, and re-layouts  1.69 us

profile of v3, /device:TPU:0, one launch (start us, length us, event | category | flops | bytes accessed | tf_op | source)
XLA Modules:
  0.0 77.6 jit_solution(3323190205074742683)
XLA Ops:
  0.0 75.9 %shard_map.73 = bf16[48,3072]{1,0:T(8,128)(2,1)} custom-call(bf16[48,3072]{1,0:T(8,128)(2,1)} %tok_ref.1, f32[1,3072]{1,0:T(1,128)} %bitcast.4, f32[1,3072]{1,0:T(1,128)} %bitcast.5, bf16[3072,3072]{1,0:T(8,128)(2,1)} %w1_hbm.1, f32[1,3072]{1,0:T(1,128)} %bitcast.6, bf16[3072,3072]{1,0:T(8,128)(2,1)} %w2_hbm.1, f32[1,3072]{1,0:T(1,128)} %bitcast.7), custom_call_target="tpu_custom_call" | custom-call | flops 14495514624 | bytes 37748736 | tf_op jit(solution)/shard_map/pallas_call | solution.py:369
  75.9 1.7 %copy.9 = bf16[48,3072]{1,0:T(8,128)(2,1)} copy(bf16[48,3072]{1,0:T(8,128)(2,1)} %shard_map.73) | data formatting | bytes 589824
